TPU v7x, 512 devices: a whole 4x8x8 slice. The times are simulated.
512 devices in a mesh: rep: 32 (over x, y), shard: 16 (over z, core).
Axes of the slice: x: 4, y: 8, z: 8, core: 2. Of those that a mesh axis runs over, the one named last changes fastest.
Arguments:
- token_pool: bfloat16 [32, 384, 2048], P('rep'), may hold values from -6 to 6
- row_index: int32 [32, 8, 1, 512], P('rep'), may hold values from 0 to 383
- weights: bfloat16 [1, 2048, 4096], P(None, None, 'shard'), may hold values from -4 to 4
- targets: bfloat16 [32, 1, 512, 4096], P('rep', None, None, 'shard'), may hold values from -2 to 2
Outputs:
- new_weights: bfloat16 [1, 2048, 4096], P(None, None, 'shard')
All inputs are finite; a program needn't handle non-finite values.
Results may differ from a plain program's by a relative error of at most 0.013.
Values may be sent and summed in bfloat16 or wider, within the bound.
A program may use at most 64 MiB of HBM per device.

v0:
```python
import math

import jax
import jax.numpy as jnp
from jax import lax
from jax.sharding import PartitionSpec as P

STEPS = 4
CUT = 2


LEARN_RATE = 0.3
MOMENTUM = 0.9
EPSILON = 1e-06


def swapped(shard, axis, apart):
    return lax.ppermute(shard, axis, [(i, i ^ 1 << apart) for i in range(lax.axis_size(axis))])


def local_steps(pool_rows, indices, goals, start_weights):
    running = start_weights.astype(jnp.float32)
    velocity = jnp.zeros_like(running)
    inv_width = 1.0 / math.sqrt(pool_rows.shape[1])
    batch_rows = indices.shape[0] // STEPS
    inv_batch = 1.0 / math.sqrt(batch_rows)
    for step_index in range(STEPS):
        picked = indices[step_index * batch_rows : (step_index + 1) * batch_rows]
        inputs = jnp.take(pool_rows, picked, axis=0)
        wanted = goals[step_index * batch_rows : (step_index + 1) * batch_rows].astype(jnp.float32)
        hidden = (
            jnp.dot(inputs, running.astype(jnp.bfloat16), preferred_element_type=jnp.float32)
            * inv_width
        )
        sigma = jax.nn.sigmoid(hidden)
        slope = sigma * (1.0 + hidden * (1.0 - sigma))
        grad_hidden = ((hidden * sigma - wanted) * slope).astype(jnp.bfloat16)
        gradient = jnp.dot(inputs.T, grad_hidden, preferred_element_type=jnp.float32) * inv_batch
        velocity = MOMENTUM * velocity + gradient
        running = running - LEARN_RATE * velocity
    return (running - start_weights.astype(jnp.float32)).astype(jnp.bfloat16)


def pair_coefs(cross_total, left_total, right_total):
    left_coef = 1.0 - cross_total / (2.0 * (left_total + EPSILON))
    right_coef = 1.0 - cross_total / (2.0 * (right_total + EPSILON))
    return (left_coef, right_coef)


def halving_combine(delta, rep_place, levels, column_group, group_count):
    current = delta.astype(jnp.float32)
    for level_index in range(levels):
        half_rows = current.shape[0] // 2
        upper = rep_place >> level_index & 1
        kept = lax.dynamic_slice_in_dim(current, upper * half_rows, half_rows, 0)
        outgoing = lax.dynamic_slice_in_dim(current, (1 - upper) * half_rows, half_rows, 0)
        incoming = swapped(outgoing, "rep", level_index)
        cross = jnp.sum(kept * incoming)
        own_square = jnp.sum(kept * kept)
        other_square = jnp.sum(incoming * incoming)
        lower_side = upper == 0
        left_square = jnp.where(lower_side, own_square, other_square)
        right_square = jnp.where(lower_side, other_square, own_square)
        rep_groups = lax.axis_size("rep") >> level_index + 1
        rep_marks = jnp.arange(rep_groups, dtype=jnp.int32) == rep_place >> level_index + 1
        column_marks = jnp.arange(group_count, dtype=jnp.int32) == column_group
        marker = (rep_marks[:, None] & column_marks[None, :]).astype(jnp.float32)
        summed = lax.psum(
            (cross * marker, left_square * marker, right_square * marker), ("rep", "shard")
        )
        cross_total = jnp.sum(summed[0] * marker)
        left_total = jnp.sum(summed[1] * marker)
        right_total = jnp.sum(summed[2] * marker)
        left_coef, right_coef = pair_coefs(cross_total, left_total, right_total)
        kept_coef = jnp.where(lower_side, left_coef, right_coef)
        incoming_coef = jnp.where(lower_side, right_coef, left_coef)
        current = kept_coef * kept + incoming_coef * incoming
    return current.astype(jnp.bfloat16)


def reversed_order(gathered, levels):
    segment_rows = gathered.shape[0] >> levels
    shaped = gathered.reshape((2,) * levels + (segment_rows, gathered.shape[1]))
    order = tuple(range(levels - 1, -1, -1)) + (levels, levels + 1)
    return jnp.transpose(shaped, order).reshape(gathered.shape)


def body(token_pool, row_index, weights, targets):
    rep_count = lax.axis_size("rep")
    levels = rep_count.bit_length() - 1
    rep_place = lax.axis_index("rep")
    column_group = lax.axis_index("shard") // CUT
    group_count = lax.axis_size("shard") // CUT
    pool_rows = token_pool[0]
    chosen_rows = lax.dynamic_index_in_dim(row_index[0], column_group, 0, keepdims=False)
    start_weights = weights[0]
    delta = local_steps(pool_rows, chosen_rows[0], targets[0, 0], start_weights)
    segment = halving_combine(delta, rep_place, levels, column_group, group_count)
    gathered = lax.all_gather(segment, "rep", axis=0, tiled=True)
    gathered = reversed_order(gathered, levels)
    results = [
        (start_weights.astype(jnp.float32) + gathered.astype(jnp.float32)).astype(jnp.bfloat16)
    ]
    return jnp.stack(results, 0)


def solution(mesh):
    in_specs = (
        P("rep", None, None),
        P("rep", None, None, None),
        P(None, None, "shard"),
        P("rep", None, None, "shard"),
    )
    out_specs = P(None, None, "shard")
    return jax.shard_map(body, mesh=mesh, in_specs=in_specs, out_specs=out_specs, check_vma=False)
```

profile of v0, /device:TPU:448, one launch (start us, length us, event | category | flops | bytes accessed | tf_op | source)
XLA Modules:
  0.0 735.0 jit_solution(17388510772092777284)
XLA Ops:
  12.4 1.8 gather_fusion.3
  14.2 2.3 fusion.17
  16.5 5.0 fusion.5
  21.5 5.4 fusion.4
  26.9 8.1 %fusion.7 = f32[2048,256]{1,0:T(8,128)} fusion(f32[2048,256]{1,0:T(8,128)} %fusion.4, bf16[1,2048,256]{2,1,0:T(8,128)(2,1)S(1)} %copy-done.1, bf16[128,2048]{1,0:T(8,128)(2,1)} %gather_fusion.3, pred[128]{0:T(512)(128)(4,1)S(1)} %get-tuple-element.53, f32[2048,256]{1,0:T(8,128)} %fusion.5, f32[2048,256]{1,0:T(8,128)} %fusion.17, ...), kind=kOutput, calls=%fused_computation.15 | convolution fusion | flops 281444352 | bytes 17892352 | tf_op jit(solution)/shard_map/dot_general | solution.py:38
  35.0 2.3 constant_dynamic-slice_fusion.7
  37.2 3.5 collective-permute-start
  40.8 23.6 %collective-permute-done = f32[1024,256]{1,0:T(8,128)} collective-permute-done((f32[1024,256]{1,0:T(8,128)}, f32[1024,256]{1,0:T(8,128)}, u32[]{:S(2)}, u32[]{:S(2)}) %collective-permute-start) | collective-permute-done | bytes 1048608 | tf_op jit(solution)/shard_map/ppermute | solution.py:18
  64.3 2.4 multiply_reduce_fusion.1
  69.9 96.9 %all-reduce.4 = (f32[16,8]{0,1:T(8,128)S(1)}, f32[16,8]{0,1:T(8,128)S(1)}, f32[16,8]{0,1:T(8,128)S(1)}) all-reduce(f32[16,8]{0,1:T(8,128)S(1)} %get-tuple-element.77, f32[16,8]{0,1:T(8,128)S(1)} %get-tuple-element.78, f32[16,8]{0,1:T(8,128)S(1)} %get-tuple-element.76), channel_id=1, replica_groups=mesh['rep'=32,'shard'=16] {'rep','shard'}, use_global_device_ids=true, to_apply=%region_5.7 | all-reduce | flops 384 | bytes 3072 | tf_op jit(solution)/shard_map/psum | solution.py:68
  173.5 2.7 collective-permute-start.1
  176.2 25.2 %collective-permute-done.1 = f32[512,256]{1,0:T(8,128)S(1)} collective-permute-done((f32[512,256]{1,0:T(8,128)}, f32[512,256]{1,0:T(8,128)S(1)}, u32[]{:S(2)}, u32[]{:S(2)}) %collective-permute-start.1) | collective-permute-done | bytes 524320 | tf_op jit(solution)/shard_map/ppermute | solution.py:18
  201.4 2.1 multiply_reduce_fusion.4
  206.7 94.7 %all-reduce.3 = (f32[8,8]{1,0:T(8,128)S(1)}, f32[8,8]{1,0:T(8,128)S(1)}, f32[8,8]{1,0:T(8,128)S(1)}) all-reduce(f32[8,8]{1,0:T(8,128)S(1)} %get-tuple-element.75, f32[8,8]{1,0:T(8,128)S(1)} %get-tuple-element.74, f32[8,8]{1,0:T(8,128)S(1)} %get-tuple-element.73), channel_id=1, replica_groups=mesh['rep'=32,'shard'=16] {'rep','shard'}, use_global_device_ids=true, to_apply=%region_14.16 | all-reduce | flops 192 | bytes 1536 | tf_op jit(solution)/shard_map/psum | solution.py:68
  306.7 5.7 collective-permute-start.2
  312.5 13.9 %collective-permute-done.2 = f32[256,256]{1,0:T(8,128)S(1)} collective-permute-done((f32[256,256]{1,0:T(8,128)}, f32[256,256]{1,0:T(8,128)S(1)}, u32[]{:S(2)}, u32[]{:S(2)}) %collective-permute-start.2) | collective-permute-done | bytes 262176 | tf_op jit(solution)/shard_map/ppermute | solution.py:18
  330.5 94.5 %all-reduce.2 = (f32[4,8]{1,0:T(4,128)S(1)}, f32[4,8]{1,0:T(4,128)S(1)}, f32[4,8]{1,0:T(4,128)S(1)}) all-reduce(f32[4,8]{1,0:T(4,128)S(1)} %get-tuple-element.71, f32[4,8]{1,0:T(4,128)S(1)} %get-tuple-element.72, f32[4,8]{1,0:T(4,128)S(1)} %get-tuple-element.70), channel_id=1, replica_groups=mesh['rep'=32,'shard'=16] {'rep','shard'}, use_global_device_ids=true, to_apply=%region_23.25 | all-reduce | flops 96 | bytes 768 | tf_op jit(solution)/shard_map/psum | solution.py:68
  429.3 3.1 collective-permute-start.3
  432.4 4.0 collective-permute-done.3
  440.3 93.8 %all-reduce.1 = (f32[2,8]{1,0:T(2,128)S(1)}, f32[2,8]{1,0:T(2,128)S(1)}, f32[2,8]{1,0:T(2,128)S(1)}) all-reduce(f32[2,8]{1,0:T(2,128)S(1)} %get-tuple-element.68, f32[2,8]{1,0:T(2,128)S(1)} %get-tuple-element.69, f32[2,8]{1,0:T(2,128)S(1)} %get-tuple-element.67), channel_id=1, replica_groups=mesh['rep'=32,'shard'=16] {'rep','shard'}, use_global_device_ids=true, to_apply=%region_32.34 | all-reduce | flops 48 | bytes 384 | tf_op jit(solution)/shard_map/psum | solution.py:68
  537.4 3.1 collective-permute-start.4
  540.5 4.6 collective-permute-done.4
  548.9 94.2 %all-reduce = (f32[1,8]{1,0:T(1,128)S(1)}, f32[1,8]{1,0:T(1,128)S(1)}, f32[1,8]{1,0:T(1,128)S(1)}) all-reduce(f32[1,8]{1,0:T(1,128)S(1)} %get-tuple-element.80, f32[1,8]{1,0:T(1,128)S(1)} %get-tuple-element.79, f32[1,8]{1,0:T(1,128)S(1)} %get-tuple-element.51), channel_id=1, replica_groups=mesh['rep'=32,'shard'=16] {'rep','shard'}, use_global_device_ids=true, to_apply=%region_41.43 | all-reduce | flops 24 | bytes 192 | tf_op jit(solution)/shard_map/psum | solution.py:68
  646.9 78.1 %all-gather.2.cloned.1.call-done = bf16[2048,256]{1,0:T(8,128)(2,1)} async-done(((bf16[64,256]{1,0:T(8,128)(2,1)}), bf16[2048,256]{1,0:T(8,128)(2,1)}) %all-gather.2.cloned.1.call-update) | async-done | bytes 1048592 | tf_op jit(solution)/shard_map/all_gather | solution.py:99
  (53 shorter events, 25.3 us)
Async XLA Ops:
  6.5 1.5 copy-start
  6.5 718.5 %all-gather.2.cloned.1.call-start = ((), (), s32[]{:S(2)}) async-start(), calls=%async_computation | async-start | bytes 1081344 | tf_op jit(solution)/shard_map/all_gather | solution.py:99
  12.4 1.8 copy-start.1
  12.4 1.8 copy-start.6
  16.5 5.0 copy-start.3
  37.2 27.1 %collective-permute-start = (f32[1024,256]{1,0:T(8,128)}, f32[1024,256]{1,0:T(8,128)}, u32[]{:S(2)}, u32[]{:S(2)}) collective-permute-start(f32[1024,256]{1,0:T(8,128)} %constant_dynamic-slice_fusion.7), channel_id=1, source_target_pairs={{0,16},{16,0},{32,48},{48,32},{64,80},{80,64},{96,112},{112,96},{1... | collective-permute-start | bytes 3145736 | tf_op jit(solution)/shard_map/ppermute | solution.py:18
  171.7 1.0 copy-start.2
  173.5 27.9 %collective-permute-start.1 = (f32[512,256]{1,0:T(8,128)}, f32[512,256]{1,0:T(8,128)S(1)}, u32[]{:S(2)}, u32[]{:S(2)}) collective-permute-start(f32[512,256]{1,0:T(8,128)} %constant_dynamic-slice_fusion.6), channel_id=1, source_target_pairs={{0,32},{16,48},{32,0},{48,16},{64,96},{80,112},{96,64},{112,80},{1... | collective-permute-start | bytes 1572872 | tf_op jit(solution)/shard_map/ppermute | solution.py:18
  201.3 103.4 %copy-start.4 = (f32[512,256]{1,0:T(8,128)}, f32[512,256]{1,0:T(8,128)S(1)}, u32[]{:S(2)}) copy-start(f32[512,256]{1,0:T(8,128)S(1)} %collective-permute-done.1) | copy-start | bytes 1572868
  306.7 19.7 %collective-permute-start.2 = (f32[256,256]{1,0:T(8,128)}, f32[256,256]{1,0:T(8,128)S(1)}, u32[]{:S(2)}, u32[]{:S(2)}) collective-permute-start(f32[256,256]{1,0:T(8,128)} %constant_dynamic-slice_fusion.5), channel_id=1, source_target_pairs={{0,64},{16,80},{32,96},{48,112},{64,0},{80,16},{96,32},{112,48},{1... | collective-permute-start | bytes 786440 | tf_op jit(solution)/shard_map/ppermute | solution.py:18
  326.4 101.8 %copy-start.5 = (f32[256,256]{1,0:T(8,128)}, f32[256,256]{1,0:T(8,128)S(1)}, u32[]{:S(2)}) copy-start(f32[256,256]{1,0:T(8,128)S(1)} %collective-permute-done.2) | copy-start | bytes 786436
  429.3 7.1 collective-permute-start.3
  537.4 7.7 %collective-permute-start.4 = (f32[64,256]{1,0:T(8,128)S(1)}, f32[64,256]{1,0:T(8,128)S(1)}, u32[]{:S(2)}, u32[]{:S(2)}) collective-permute-start(f32[64,256]{1,0:T(8,128)S(1)} %constant_dynamic-slice_fusion.3), channel_id=1, source_target_pairs={{0,256},{16,272},{32,288},{48,304},{64,320},{80,336},{96,352},{112... | collective-permute-start | bytes 196616 | tf_op jit(solution)/shard_map/ppermute | solution.py:18
Sparse Core Ops, SparseCore 0:
  647.0 77.9 all-gather.1
where the time goes:
time: 741 us; the launch traced here: 735 us
  blocking collectives  474 us (64%)
  waiting for transfers between devices  149 us (20%)
  between operations  38.8 us (5%)
  other arithmetic  22 us (3%)
  matrix products  20.8 us (3%)
  starting transfers between devices  18.1 us (2%)
  local copies, waits for them, and re-layouts  11.8 us (2%)
    psum x5, blocking collectives, halving_combine(): lax.psum((cross * marker, left_square * marker, right_square * marker), (...  474 us
    all_gather x1, waiting for transfers between devices, body(): gathered = lax.all_gather(segment, 'rep', axis=0, tiled=True)  78.1 us
    ppermute x5, waiting for transfers between devices, swapped(): lax.ppermute(shard, axis, [(i, i ^ 1 << apart) for i in range(lax.axis_si...  71.2 us
    dot_general x4, matrix products, local_steps(): jnp.dot(inputs.T, grad_hidden, preferred_element_type=jnp.float32)  20.8 us
    ppermute x5, starting transfers between devices, swapped(): lax.ppermute(shard, axis, [(i, i ^ 1 << apart) for i in range(lax.axis_si...  18.1 us
  transfers between devices with their start and end apart: 6, of which 6 were waited for; matrix products, arithmetic and copies ran while one was open for 0% of the time, Pallas kernels for 0%

commit v1 on v0

v1 whole, which is shorter than its diff:
```python
import functools
import math

import jax
import jax.numpy as jnp
from jax import lax
from jax.experimental import pallas as pl
from jax.experimental.pallas import tpu as pltpu
from jax.sharding import PartitionSpec as P

STEPS = 4
CUT = 2
RING = 8

LEARN_RATE = 0.3
MOMENTUM = 0.9
EPSILON = 1e-06

MESH = pl.DeviceIdType.MESH
F32 = jnp.float32
BF16 = jnp.bfloat16
A_ROWS = 48


def dot(a, b):
    return jnp.dot(a, b, preferred_element_type=F32)


def dot_last(a, b):
    return lax.dot_general(a, b, (((1,), (1,)), ((), ())), preferred_element_type=F32)


def dot_first(a, b):
    return lax.dot_general(a, b, (((0,), (0,)), ((), ())), preferred_element_type=F32)


def local_steps(pool, start, picked, goals):
    pool_count, width = pool.shape
    total = picked.shape[1]
    rows = total // STEPS
    inv_width = 1.0 / math.sqrt(width)
    scale = LEARN_RATE / math.sqrt(rows)
    first = dot(pool, start)
    kernel_matrix = dot_last(pool, pool).astype(BF16)
    slots = lax.broadcasted_iota(jnp.int32, (pool_count, total), 0)
    marks = (slots == picked).astype(BF16)
    z = first
    velocity = None
    moved = None
    for step in range(STEPS):
        mark = marks[:, step * rows : (step + 1) * rows]
        high = z.astype(BF16)
        low = (z - high.astype(F32)).astype(BF16)
        hidden = (dot_first(mark, high) + dot_first(mark, low)) * inv_width
        sigma = jax.nn.sigmoid(hidden)
        slope = sigma * (1.0 + hidden * (1.0 - sigma))
        wanted = goals[step * rows : (step + 1) * rows].astype(F32)
        grad_hidden = ((hidden * sigma - wanted) * slope).astype(BF16)
        spread = dot(mark, grad_hidden)
        velocity = spread if velocity is None else MOMENTUM * velocity + spread
        moved = velocity if moved is None else moved + velocity
        if step < STEPS - 1:
            z = first - scale * dot(kernel_matrix, moved.astype(BF16))
    return (-scale * moved).astype(BF16)


def tree_coefs(gram):
    count, lanes = gram.shape
    row = lax.broadcasted_iota(jnp.int32, gram.shape, 0)
    lane = lax.broadcasted_iota(jnp.int32, gram.shape, 1)
    own = row == lane
    coef = jnp.ones((count, 1), F32)
    bit = 1
    while bit < count:
        partner = lane == (row ^ bit)
        squares = jnp.where(own, gram, 0.0)
        crosses = jnp.where(partner, gram, 0.0)
        gains = []
        for axis in (1, 0):
            square = jnp.maximum(jnp.sum(squares, axis=axis, keepdims=True), 0.0)
            cross = jnp.sum(crosses, axis=axis, keepdims=True)
            gains.append(1.0 - cross / (2.0 * (square + EPSILON)))
        coef = coef * gains[0]
        gram = gram * gains[0] * gains[1]
        gram = gram + jnp.where(
            (lane & bit) == 0, pltpu.roll(gram, lanes - bit, 1), pltpu.roll(gram, bit, 1)
        )
        gram = gram + jnp.where(
            (row & bit) == 0, pltpu.roll(gram, count - bit, 0), pltpu.roll(gram, bit, 0)
        )
        bit *= 2
    return coef


def kernel(
    pool_ref,
    index_ref,
    start_ref,
    goal_ref,
    out_ref,
    turned,
    delta,
    recv,
    wide,
    gram_pad,
    gram_one,
    gram_two,
    coefs,
    a2a_send,
    a2a_recv,
    one_send,
    one_recv,
    two_send,
    two_recv,
    ya_send,
    ya_recv,
    xa_send,
    xa_recv,
    xb_send,
    xb_recv,
    yb_send,
    yb_recv,
):
    reps = recv.shape[0]
    seg = recv.shape[1]
    cols = recv.shape[2]
    tall = reps // RING
    me = lax.axis_index("rep")
    shard = lax.axis_index("shard")
    x = me // RING
    y = me % RING
    core = shard % CUT

    barrier = pltpu.get_barrier_semaphore()

    def greet(k, carry):
        pl.semaphore_signal(
            barrier,
            inc=1,
            device_id={"rep": lax.rem(me + k, reps), "shard": shard},
            device_id_type=MESH,
        )
        return carry

    def greet_other(k, carry):
        pl.semaphore_signal(
            barrier,
            inc=1,
            device_id={"rep": x * RING + lax.rem(y + k, RING), "shard": shard ^ 1},
            device_id_type=MESH,
        )
        return carry

    lax.fori_loop(1, reps, greet, 0)
    lax.fori_loop(0, RING, greet_other, 0)

    pool = pool_ref[0]
    turned[...] = pool.T
    picked = index_ref[0, pl.ds(shard // CUT, 1), 0, :]
    weights = local_steps(pool, start_ref[0], picked, goal_ref[0, 0])

    pl.semaphore_wait(barrier, reps - 1 + RING)

    def a2a(peer):
        return pltpu.make_async_remote_copy(
            src_ref=delta.at[pl.ds(pl.multiple_of(peer * seg, seg), seg), :],
            dst_ref=recv.at[me],
            send_sem=a2a_send.at[peer],
            recv_sem=a2a_recv.at[me],
            device_id={"rep": peer, "shard": shard},
            device_id_type=MESH,
        )

    def a2a_arrival(peer):
        return pltpu.make_async_remote_copy(
            src_ref=delta.at[pl.ds(0, seg), :],
            dst_ref=recv.at[peer],
            send_sem=a2a_send.at[peer],
            recv_sem=a2a_recv.at[peer],
            device_id={"rep": peer, "shard": shard},
            device_id_type=MESH,
        )

    for i in range(tall):
        to_x = lax.rem(x + i, tall)
        base = pl.multiple_of(to_x * RING * seg, RING * seg)
        block = pl.ds(base, RING * seg)
        delta[block, :] = dot(turned[block, :], weights).astype(BF16)

        def send(j, carry, to_x=to_x):
            a2a(to_x * RING + lax.rem(y + j, RING)).start()
            return carry

        lax.fori_loop(1 if i == 0 else 0, RING, send, 0)
    recv[me] = delta[pl.ds(pl.multiple_of(me * seg, seg), seg), :]

    def arrive(k, carry):
        a2a_arrival(lax.rem(me + k, reps)).wait_recv()
        return carry

    lax.fori_loop(1, reps, arrive, 0)

    def widen(q, carry):
        for h in range(cols // 128):
            wide[h, pl.ds(pl.multiple_of(q * seg, seg), seg), :] = recv[
                q, :, 128 * h : 128 * h + 128
            ].astype(F32)
        return carry

    lax.fori_loop(0, reps, widen, 0)

    def add_row(r, total):
        for h in range(cols // 128):
            parts = wide[h, pl.ds(r, reps, stride=seg), :].astype(BF16)
            total = total + dot_last(parts, parts)
        return total

    gram = lax.fori_loop(0, seg, add_row, jnp.zeros((reps, reps), F32))
    gram_pad[...] = jnp.zeros_like(gram_pad)
    gram_pad[:, 0:reps] = gram
    packed = gram_pad[0:8, :]
    for k in range(1, reps // 8):
        packed = packed + pltpu.roll(gram_pad[8 * k : 8 * k + 8, :], reps * k, 1)

    mine = y * CUT + core
    gram_one[mine] = packed

    def one(k, arriving):
        peer = lax.rem(mine + k, RING * CUT)
        place = peer if arriving else mine
        return pltpu.make_async_remote_copy(
            src_ref=gram_one.at[mine],
            dst_ref=gram_one.at[place],
            send_sem=one_send.at[peer],
            recv_sem=one_recv.at[place],
            device_id={
                "rep": x * RING + peer // CUT,
                "shard": (shard // CUT) * CUT + peer % CUT,
            },
            device_id_type=MESH,
        )

    def one_start(k, carry):
        one(k, False).start()
        return carry

    def one_wait(k, carry):
        one(k, True).wait_recv()
        return carry

    lax.fori_loop(1, RING * CUT, one_start, 0)
    lax.fori_loop(1, RING * CUT, one_wait, 0)
    gram_two[x] = jnp.sum(gram_one[...], axis=0)

    def x_peer(i):
        return lax.rem(x + i, tall)

    def copy(src, dst, send_sem, recv_sem, rep):
        return pltpu.make_async_remote_copy(
            src_ref=src,
            dst_ref=dst,
            send_sem=send_sem,
            recv_sem=recv_sem,
            device_id={"rep": rep, "shard": shard},
            device_id_type=MESH,
        )

    for i in range(1, tall):
        p = x_peer(i)
        copy(gram_two.at[x], gram_two.at[x], two_send.at[p], two_recv.at[x], p * RING + y).start()
    for i in range(1, tall):
        p = x_peer(i)
        copy(gram_two.at[x], gram_two.at[p], two_send.at[p], two_recv.at[p], p * RING + y).wait_recv()
    packed = jnp.sum(gram_two[...], axis=0)
    lane = lax.broadcasted_iota(jnp.int32, packed.shape, 1)
    pieces = [
        jnp.where(lane < reps, packed if k == 0 else pltpu.roll(packed, 128 - reps * k, 1), 0.0)
        for k in range(reps // 8)
    ]
    gram_pad[...] = jnp.concatenate(pieces, axis=0)
    coefs[...] = jnp.broadcast_to(tree_coefs(gram_pad[...]), coefs.shape)

    def combine(q, total):
        return total + coefs[pl.ds(q, 1), :] * recv[q].astype(F32)

    combined = lax.fori_loop(0, reps, combine, jnp.zeros((seg, cols), F32)).astype(BF16)
    before = start_ref[0, pl.ds(pl.multiple_of(me * seg, seg), seg), :]
    out_ref[x, y] = (before.astype(F32) + combined.astype(F32)).astype(BF16)

    top = pl.ds(0, A_ROWS)
    low = pl.ds(A_ROWS, seg - A_ROWS)

    def y_peer(j):
        return lax.rem(y + j, RING)

    def ya(j, arriving):
        p = y_peer(j)
        return copy(
            out_ref.at[x, y, top],
            out_ref.at[x, p if arriving else y, top],
            ya_send.at[p],
            ya_recv.at[p if arriving else y],
            x * RING + p,
        )

    def xa(i, arriving):
        p = x_peer(i)
        return copy(
            out_ref.at[x, :, top],
            out_ref.at[p if arriving else x, :, top],
            xa_send.at[p],
            xa_recv.at[p if arriving else x],
            p * RING + y,
        )

    def xb(i, arriving):
        p = x_peer(i)
        return copy(
            out_ref.at[x, y, low],
            out_ref.at[p if arriving else x, y, low],
            xb_send.at[p],
            xb_recv.at[p if arriving else x],
            p * RING + y,
        )

    def yb(j, arriving):
        p = y_peer(j)
        return copy(
            out_ref.at[:, y, low],
            out_ref.at[:, p if arriving else y, low],
            yb_send.at[p],
            yb_recv.at[p if arriving else y],
            x * RING + p,
        )

    for i in range(1, tall):
        xb(i, False).start()
    for j in range(1, RING):
        ya(j, False).start()
    for i in range(1, tall):
        xb(i, True).wait_recv()
    for j in range(1, RING):
        yb(j, False).start()
    for j in range(1, RING):
        ya(j, True).wait_recv()
    for i in range(1, tall):
        xa(i, False).start()
    for j in range(1, RING):
        yb(j, True).wait_recv()
    for i in range(1, tall):
        xa(i, True).wait_recv()

    def a2a_left(k, carry):
        a2a(lax.rem(me + k, reps)).wait_send()
        return carry

    def one_left(k, carry):
        one(k, False).wait_send()
        return carry

    lax.fori_loop(1, reps, a2a_left, 0)
    lax.fori_loop(1, RING * CUT, one_left, 0)
    for i in range(1, tall):
        p = x_peer(i)
        copy(gram_two.at[x], gram_two.at[x], two_send.at[p], two_recv.at[x], p * RING + y).wait_send()
        xa(i, False).wait_send()
        xb(i, False).wait_send()
    for j in range(1, RING):
        ya(j, False).wait_send()
        yb(j, False).wait_send()


def body(token_pool, row_index, weights, targets):
    reps = lax.axis_size("rep")
    tall = reps // RING
    pool_count, width = token_pool.shape[1:]
    cols = weights.shape[2]
    seg = width // reps
    dma = pltpu.SemaphoreType.DMA
    out = pl.pallas_call(
        kernel,
        out_shape=jax.ShapeDtypeStruct((tall, RING, seg, cols), BF16),
        in_specs=[pl.BlockSpec(memory_space=pltpu.VMEM)] * 4,
        out_specs=pl.BlockSpec(memory_space=pltpu.VMEM),
        scratch_shapes=[
            pltpu.VMEM((width, pool_count), BF16),
            pltpu.VMEM((width, cols), BF16),
            pltpu.VMEM((reps, seg, cols), BF16),
            pltpu.VMEM((cols // 128, reps * seg, 128), F32),
            pltpu.VMEM((reps, 128), F32),
            pltpu.VMEM((RING * CUT, 8, 128), F32),
            pltpu.VMEM((tall, 8, 128), F32),
            pltpu.VMEM((reps, cols), F32),
            dma((reps,)),
            dma((reps,)),
            dma((RING * CUT,)),
            dma((RING * CUT,)),
            dma((tall,)),
            dma((tall,)),
            dma((RING,)),
            dma((RING,)),
            dma((tall,)),
            dma((tall,)),
            dma((tall,)),
            dma((tall,)),
            dma((RING,)),
            dma((RING,)),
        ],
        compiler_params=pltpu.CompilerParams(
            collective_id=0, has_side_effects=True, vmem_limit_bytes=40 * 1024 * 1024
        ),
    )(token_pool, row_index, weights, targets)
    return out.reshape(weights.shape)


def solution(mesh):
    in_specs = (
        P("rep", None, None),
        P("rep", None, None, None),
        P(None, None, "shard"),
        P("rep", None, None, "shard"),
    )
    out_specs = P(None, None, "shard")
    return jax.shard_map(body, mesh=mesh, in_specs=in_specs, out_specs=out_specs, check_vma=False)
```

time: 741 us -> 81.3 us (0.11)
  blocking collectives: 474 us -> 0 us
  waiting for transfers between devices: 149 us -> 0 us
  Pallas kernels: 0 us -> 75.8 us
  between operations: 38.8 us -> 0.01 us
  other arithmetic: 22 us -> 0 us
  matrix products: 20.8 us -> 0 us
  starting transfers between devices: 18.1 us -> 0 us
    psum x5 -> x0, blocking collectives: 474 us -> none  [halving_combine(): lax.psum((cross * marker, left_square * marker, right_square * marker), (...]
    all_gather x1 -> x0, waiting for transfers between devices: 78.1 us -> none  [body(): gathered = lax.all_gather(segment, 'rep', axis=0, tiled=True)]
    pallas_call x0 -> x1, Pallas kernels: none -> 75.8 us  [body(): pl.pallas_call(kernel, out_shape=jax.ShapeDtypeStruct((tall, RING, seg, c...]
    ppermute x5 -> x0, waiting for transfers between devices: 71.2 us -> none  [swapped(): lax.ppermute(shard, axis, [(i, i ^ 1 << apart) for i in range(lax.axis_si...]
    dot_general x4 -> x0, matrix products: 20.8 us -> none  [local_steps(): jnp.dot(inputs.T, grad_hidden, preferred_element_type=jnp.float32)]
    ppermute x5 -> x0, starting transfers between devices: 18.1 us -> none  [swapped(): lax.ppermute(shard, axis, [(i, i ^ 1 << apart) for i in range(lax.axis_si...]
    reduce_sum x10 -> x0, other arithmetic: 10.3 us -> none  [the longest x5 6.66 us: halving_combine(): own_square = jnp.sum(kept * kept)]
  transfers between devices with their start and end apart: 6 -> 0, of which waited for: 6 -> 0; matrix products, arithmetic and copies ran while one was open for 0% -> 0% of each run, Pallas kernels for 0% -> 0%
where the time goes in v1:
time: 81.3 us; the launch traced here: 81.1 us
  Pallas kernels  75.8 us (93%)
  local copies, waits for them, and re-layouts  5.27 us (6%)
    pallas_call x1, Pallas kernels, body(): pl.pallas_call(kernel, out_shape=jax.ShapeDtypeStruct((tall, RING, seg, c...  75.8 us
    unnamed x9, local copies, waits for them, and re-layouts  5.27 us

profile of v1, /device:TPU:448, one launch (start us, length us, event | category | flops | bytes accessed | tf_op | source)
XLA Modules:
  0.0 81.1 jit_solution(14115036808036933980)
XLA Ops:
  0.0 0.0 copy-start
  0.0 1.4 %copy-done = bf16[1,384,2048]{2,1,0:T(8,128)(2,1)S(1)} copy-done((bf16[1,384,2048]{2,1,0:T(8,128)(2,1)S(1)}, bf16[1,384,2048]{2,1,0:T(8,128)(2,1)}, u32[]{:S(2)}) %copy-start) | copy-done | bytes 1572888
  1.4 0.0 copy-start.1
  1.4 1.2 %copy-done.1 = bf16[1,2048,256]{2,1,0:T(8,128)(2,1)S(1)} copy-done((bf16[1,2048,256]{2,1,0:T(8,128)(2,1)S(1)}, bf16[1,2048,256]{2,1,0:T(8,128)(2,1)}, u32[]{:S(2)}) %copy-start.1) | copy-done | bytes 1048600
  2.6 0.0 copy-start.2
  2.6 0.9 %copy-done.2 = bf16[1,1,512,256]{3,2,1,0:T(8,128)(2,1)S(1)} copy-done((bf16[1,1,512,256]{3,2,1,0:T(8,128)(2,1)S(1)}, bf16[1,1,512,256]{3,2,1,0:T(8,128)(2,1)}, u32[]{:S(2)}) %copy-start.2) | copy-done | bytes 262168
  3.6 0.0 copy-start.3
  3.6 0.7 copy-done.3
  4.3 75.8 %shard_map.46 = bf16[4,8,64,256]{3,2,1,0:T(8,128)(2,1)S(1)} custom-call(bf16[1,384,2048]{2,1,0:T(8,128)(2,1)S(1)} %copy-done, s32[1,8,1,512]{3,2,1,0:T(1,128)S(1)} %copy-done.3, bf16[1,2048,256]{2,1,0:T(8,128)(2,1)S(1)} %copy-done.1, bf16[1,1,512,256]{3,2,1,0:T(8,128)(2,1)S(1)} %copy-done.2), custom_call_target="tpu_custom_call" | custom-call | tf_op jit(solution)/shard_map/pallas_call | solution.py:380
  80.1 1.0 %copy.6 = bf16[1,2048,256]{2,1,0:T(8,128)(2,1)} copy(bf16[1,2048,256]{2,1,0:T(8,128)(2,1)S(1)} %bitcast.1) | data formatting | bytes 2097152
Async XLA Ops:
  0.0 1.4 %copy-start = (bf16[1,384,2048]{2,1,0:T(8,128)(2,1)S(1)}, bf16[1,384,2048]{2,1,0:T(8,128)(2,1)}, u32[]{:S(2)}) copy-start(bf16[1,384,2048]{2,1,0:T(8,128)(2,1)} %pool_ref.1) | copy-start | bytes 4718596
  1.4 1.2 %copy-start.1 = (bf16[1,2048,256]{2,1,0:T(8,128)(2,1)S(1)}, bf16[1,2048,256]{2,1,0:T(8,128)(2,1)}, u32[]{:S(2)}) copy-start(bf16[1,2048,256]{2,1,0:T(8,128)(2,1)} %start_ref.1) | copy-start | bytes 3145732
  2.6 0.9 %copy-start.2 = (bf16[1,1,512,256]{3,2,1,0:T(8,128)(2,1)S(1)}, bf16[1,1,512,256]{3,2,1,0:T(8,128)(2,1)}, u32[]{:S(2)}) copy-start(bf16[1,1,512,256]{3,2,1,0:T(8,128)(2,1)} %goal_ref.1) | copy-start | bytes 786436
  3.6 0.7 copy-start.3

commit v2 on v1

v2 whole, which is shorter than its diff:
```python
import functools
import math

import jax
import jax.numpy as jnp
from jax import lax
from jax.experimental import pallas as pl
from jax.experimental.pallas import tpu as pltpu
from jax.sharding import PartitionSpec as P

STEPS = 4
CUT = 2
RING = 8

LEARN_RATE = 0.3
MOMENTUM = 0.9
EPSILON = 1e-06

MESH = pl.DeviceIdType.MESH
F32 = jnp.float32
BF16 = jnp.bfloat16
A_ROWS = 48


def dot(a, b):
    return jnp.dot(a, b, preferred_element_type=F32)


def dot_last(a, b):
    return lax.dot_general(a, b, (((1,), (1,)), ((), ())), preferred_element_type=F32)


def dot_first(a, b):
    return lax.dot_general(a, b, (((0,), (0,)), ((), ())), preferred_element_type=F32)


def local_steps(pool, start, picked, goals):
    pool_count, width = pool.shape
    total = picked.shape[1]
    rows = total // STEPS
    inv_width = 1.0 / math.sqrt(width)
    scale = LEARN_RATE / math.sqrt(rows)
    first = dot(pool, start)
    kernel_matrix = dot_last(pool, pool).astype(BF16)
    slots = lax.broadcasted_iota(jnp.int32, (pool_count, total), 0)
    marks = (slots == picked).astype(BF16)
    z = first
    velocity = None
    moved = None
    for step in range(STEPS):
        mark = marks[:, step * rows : (step + 1) * rows]
        high = z.astype(BF16)
        low = (z - high.astype(F32)).astype(BF16)
        hidden = (dot_first(mark, high) + dot_first(mark, low)) * inv_width
        sigma = jax.nn.sigmoid(hidden)
        slope = sigma * (1.0 + hidden * (1.0 - sigma))
        wanted = goals[step * rows : (step + 1) * rows].astype(F32)
        grad_hidden = ((hidden * sigma - wanted) * slope).astype(BF16)
        spread = dot(mark, grad_hidden)
        velocity = spread if velocity is None else MOMENTUM * velocity + spread
        moved = velocity if moved is None else moved + velocity
        if step < STEPS - 1:
            z = first - scale * dot(kernel_matrix, moved.astype(BF16))
    return (-scale * moved).astype(BF16)


def tree_coefs(gram):
    count, lanes = gram.shape
    row = lax.broadcasted_iota(jnp.int32, gram.shape, 0)
    lane = lax.broadcasted_iota(jnp.int32, gram.shape, 1)
    own = row == lane
    coef = jnp.ones((count, 1), F32)
    bit = 1
    while bit < count:
        partner = lane == (row ^ bit)
        squares = jnp.where(own, gram, 0.0)
        crosses = jnp.where(partner, gram, 0.0)
        gains = []
        for axis in (1, 0):
            square = jnp.maximum(jnp.sum(squares, axis=axis, keepdims=True), 0.0)
            cross = jnp.sum(crosses, axis=axis, keepdims=True)
            gains.append(1.0 - cross / (2.0 * (square + EPSILON)))
        coef = coef * gains[0]
        gram = gram * gains[0] * gains[1]
        gram = gram + jnp.where(
            (lane & bit) == 0, pltpu.roll(gram, lanes - bit, 1), pltpu.roll(gram, bit, 1)
        )
        gram = gram + jnp.where(
            (row & bit) == 0, pltpu.roll(gram, count - bit, 0), pltpu.roll(gram, bit, 0)
        )
        bit *= 2
    return coef


def kernel(
    pool_hbm,
    index_hbm,
    start_hbm,
    goal_hbm,
    out_ref,
    pool_ref,
    index_ref,
    start_ref,
    goal_ref,
    turned,
    delta,
    recv,
    wide,
    operand,
    gram_pad,
    gram_one,
    gram_two,
    coefs,
    load_sem,
    a2a_send,
    a2a_recv,
    one_send,
    one_recv,
    two_send,
    two_recv,
    ya_send,
    ya_recv,
    xa_send,
    xa_recv,
    xb_send,
    xb_recv,
    yb_send,
    yb_recv,
):
    halves, reps, half, cols = recv.shape
    seg = halves * half
    tall = reps // RING
    pairs = tall * CUT
    me = lax.axis_index("rep")
    shard = lax.axis_index("shard")
    x = me // RING
    y = me % RING
    core = shard % CUT

    loads = [
        pltpu.make_async_copy(src, dst, load_sem.at[k])
        for k, (src, dst) in enumerate(
            (
                (pool_hbm.at[0], pool_ref),
                (start_hbm.at[0], start_ref),
                (index_hbm.at[0, pl.ds(shard // CUT, 1), 0], index_ref),
                (goal_hbm.at[0, 0], goal_ref),
            )
        )
    ]
    for load in loads:
        load.start()

    barrier = pltpu.get_barrier_semaphore()

    def greet(k, carry):
        pl.semaphore_signal(
            barrier,
            inc=1,
            device_id={"rep": lax.rem(me + k, reps), "shard": shard},
            device_id_type=MESH,
        )
        return carry

    def greet_other(i, carry):
        pl.semaphore_signal(
            barrier,
            inc=1,
            device_id={"rep": lax.rem(x + i, tall) * RING + y, "shard": shard ^ 1},
            device_id_type=MESH,
        )
        return carry

    lax.fori_loop(1, reps, greet, 0)
    lax.fori_loop(0, tall, greet_other, 0)

    def copy(src, dst, send_sem, recv_sem, rep, to_shard=None):
        return pltpu.make_async_remote_copy(
            src_ref=src,
            dst_ref=dst,
            send_sem=send_sem,
            recv_sem=recv_sem,
            device_id={"rep": rep, "shard": shard if to_shard is None else to_shard},
            device_id_type=MESH,
        )

    def x_peer(i):
        return lax.rem(x + i, tall)

    def y_peer(j):
        return lax.rem(y + j, RING)

    loads[0].wait()
    turned[...] = pool_ref[...].T
    for load in loads[1:]:
        load.wait()
    weights = local_steps(pool_ref[...], start_ref[...], index_ref[...], goal_ref[...])

    pl.semaphore_wait(barrier, reps - 1 + tall)

    def a2a(peer, h):
        return copy(
            delta.at[pl.ds(pl.multiple_of(peer * seg + h * half, half), half), :],
            recv.at[h, me],
            a2a_send.at[0],
            a2a_recv.at[h],
            peer,
        )

    def a2a_all(h):
        count = reps - 1
        return copy(
            recv.at[h, pl.ds(0, count)],
            recv.at[h, pl.ds(0, count)],
            a2a_send.at[0],
            a2a_recv.at[h],
            lax.rem(me + 1, reps),
        )

    for i in range(tall):
        to_x = x_peer(i)
        block = pl.ds(pl.multiple_of(to_x * RING * seg, RING * seg), RING * seg)
        delta[block, :] = dot(turned[block, :], weights).astype(BF16)

        def send(j, carry, to_x=to_x):
            a2a(to_x * RING + y_peer(j), 0).start()
            return carry

        lax.fori_loop(1 if i == 0 else 0, RING, send, 0)

    def send_rest(k, carry):
        a2a(lax.rem(me + k, reps), 1).start()
        return carry

    lax.fori_loop(1, reps, send_rest, 0)
    for h in range(halves):
        own = pl.ds(pl.multiple_of(me * seg + h * half, half), half)
        recv[h, me] = delta[own, :]

    gram = None
    for h in range(halves):
        a2a_all(h).wait_recv()
        for q in range(reps):
            for c in range(cols // 128):
                wide[c, half * q : half * q + half, :] = recv[
                    h, q, :, 128 * c : 128 * c + 128
                ].astype(F32)
        for r in range(half):
            for c in range(cols // 128):
                part = wide[c, pl.ds(r, reps, stride=half), :]
                place = r * cols + 128 * c
                operand[:, place : place + 128] = part.astype(BF16)
        term = dot_last(operand[...], operand[...])
        gram = term if gram is None else gram + term

    gram_pad[...] = jnp.zeros_like(gram_pad)
    gram_pad[:, 0:reps] = gram
    packed = gram_pad[0:8, :]
    for k in range(1, reps // 8):
        packed = packed + pltpu.roll(gram_pad[8 * k : 8 * k + 8, :], reps * k, 1)

    mine = x * CUT + core
    gram_one[mine] = packed

    def one(k, arriving):
        peer = lax.rem(mine + k, pairs)
        place = peer if arriving else mine
        return copy(
            gram_one.at[mine],
            gram_one.at[place],
            one_send.at[peer],
            one_recv.at[place],
            (peer // CUT) * RING + y,
            (shard // CUT) * CUT + peer % CUT,
        )

    def two(j, arriving):
        p = y_peer(j)
        place = p if arriving else y
        return copy(
            gram_two.at[y], gram_two.at[place], two_send.at[p], two_recv.at[place], x * RING + p
        )

    far_first = (4, 3, 5, 2, 6, 1, 7)
    for k in range(1, pairs):
        one(k, False).start()
    for k in range(1, pairs):
        one(k, True).wait_recv()
    gram_two[y] = jnp.sum(gram_one[...], axis=0)
    for j in far_first:
        two(j, False).start()
    for j in range(1, RING):
        two(j, True).wait_recv()
    packed = jnp.sum(gram_two[...], axis=0)
    lane = lax.broadcasted_iota(jnp.int32, packed.shape, 1)
    pieces = [
        jnp.where(lane < reps, packed if k == 0 else pltpu.roll(packed, 128 - reps * k, 1), 0.0)
        for k in range(reps // 8)
    ]
    coef = tree_coefs(jnp.concatenate(pieces, axis=0))
    coefs[...] = jnp.broadcast_to(coef, coefs.shape)

    for h in range(halves):
        total = jnp.zeros((half, cols), F32)
        for q in range(reps):
            total = total + coefs[q : q + 1, :] * recv[h, q].astype(F32)
        rows = pl.ds(pl.multiple_of(me * seg + h * half, half), half)
        combined = total.astype(BF16).astype(F32)
        out_ref[x, y, half * h : half * h + half] = (
            start_ref[rows, :].astype(F32) + combined
        ).astype(BF16)

    top = pl.ds(0, A_ROWS)
    low = pl.ds(A_ROWS, seg - A_ROWS)

    def ya(j, arriving):
        p = y_peer(j)
        place = p if arriving else y
        return copy(
            out_ref.at[x, y, top],
            out_ref.at[x, place, top],
            ya_send.at[p],
            ya_recv.at[place],
            x * RING + p,
        )

    def xa(i, j):
        p = x_peer(i)
        chunk = out_ref.at[x, y_peer(j), top]
        return copy(chunk, chunk, xa_send.at[p], xa_recv.at[x], p * RING + y)

    def xa_all(i):
        p = x_peer(i)
        return copy(
            out_ref.at[x, :, top], out_ref.at[p, :, top], xa_send.at[p], xa_recv.at[p], p * RING + y
        )

    def xb(i, arriving):
        p = x_peer(i)
        place = p if arriving else x
        return copy(
            out_ref.at[x, y, low],
            out_ref.at[place, y, low],
            xb_send.at[p],
            xb_recv.at[place],
            p * RING + y,
        )

    def yb(j, arriving):
        p = y_peer(j)
        place = p if arriving else y
        return copy(
            out_ref.at[:, y, low],
            out_ref.at[:, place, low],
            yb_send.at[p],
            yb_recv.at[place],
            x * RING + p,
        )

    near_first = (1, 7, 2, 6, 3, 5, 4)
    across = (2, 1, 3)
    for i in across:
        xb(i, False).start()
    for j in near_first:
        ya(j, False).start()
    for i in across:
        xa(i, 0).start()
    for i in range(1, tall):
        xb(i, True).wait_recv()
    for j in far_first:
        yb(j, False).start()
    for j in near_first:
        ya(j, True).wait_recv()
        for i in across:
            xa(i, j).start()
    for j in range(1, RING):
        yb(j, True).wait_recv()
    for i in range(1, tall):
        xa_all(i).wait_recv()

    for h in range(halves):
        a2a_all(h).wait_send()
    for k in range(1, pairs):
        one(k, False).wait_send()
    for j in range(1, RING):
        two(j, False).wait_send()
        ya(j, False).wait_send()
        yb(j, False).wait_send()
    for i in range(1, tall):
        xa_all(i).wait_send()
        xb(i, False).wait_send()


def body(token_pool, row_index, weights, targets):
    reps = lax.axis_size("rep")
    tall = reps // RING
    pool_count, width = token_pool.shape[1:]
    total = row_index.shape[3]
    cols = weights.shape[2]
    seg = width // reps
    half = seg // 2
    dma = pltpu.SemaphoreType.DMA
    out = pl.pallas_call(
        kernel,
        out_shape=jax.ShapeDtypeStruct((tall, RING, seg, cols), BF16),
        in_specs=[pl.BlockSpec(memory_space=pltpu.HBM)] * 4,
        out_specs=pl.BlockSpec(memory_space=pltpu.VMEM),
        scratch_shapes=[
            pltpu.VMEM((pool_count, width), BF16),
            pltpu.VMEM((1, total), jnp.int32),
            pltpu.VMEM((width, cols), BF16),
            pltpu.VMEM((total, cols), BF16),
            pltpu.VMEM((width, pool_count), BF16),
            pltpu.VMEM((width, cols), BF16),
            pltpu.VMEM((2, reps, half, cols), BF16),
            pltpu.VMEM((cols // 128, reps * half, 128), F32),
            pltpu.VMEM((reps, half * cols), BF16),
            pltpu.VMEM((reps, 128), F32),
            pltpu.VMEM((tall * CUT, 8, 128), F32),
            pltpu.VMEM((RING, 8, 128), F32),
            pltpu.VMEM((reps, cols), F32),
            dma((4,)),
            dma((1,)),
            dma((2,)),
            dma((tall * CUT,)),
            dma((tall * CUT,)),
            dma((RING,)),
            dma((RING,)),
            dma((RING,)),
            dma((RING,)),
            dma((tall,)),
            dma((tall,)),
            dma((tall,)),
            dma((tall,)),
            dma((RING,)),
            dma((RING,)),
        ],
        compiler_params=pltpu.CompilerParams(
            collective_id=0, has_side_effects=True, vmem_limit_bytes=60 * 1024 * 1024
        ),
    )(token_pool, row_index, weights, targets)
    return out.reshape(weights.shape)


def solution(mesh):
    in_specs = (
        P("rep", None, None),
        P("rep", None, None, None),
        P(None, None, "shard"),
        P("rep", None, None, "shard"),
    )
    out_specs = P(None, None, "shard")
    return jax.shard_map(body, mesh=mesh, in_specs=in_specs, out_specs=out_specs, check_vma=False)
```

time: 81.3 us -> 64.8 us (0.80)
  the two profiles are of different devices: /device:TPU:448 before, /device:TPU:394 now
where the time goes in v2:
time: 64.8 us; the launch traced here: 64.7 us
  Pallas kernels  62.4 us (96%)
  local copies, waits for them, and re-layouts  2.26 us (3%)
    pallas_call x1, Pallas kernels, body(): pl.pallas_call(kernel, out_shape=jax.ShapeDtypeStruct((tall, RING, seg, c...  62.4 us
    unnamed x1, local copies, waits for them, and re-layouts  2.26 us

profile of v2, /device:TPU:394, one launch (start us, length us, event | category | flops | bytes accessed | tf_op | source)
XLA Modules:
  0.0 64.7 jit_solution(2317222792741125719)
XLA Ops:
  0.0 62.4 %shard_map.46 = bf16[4,8,64,256]{3,2,1,0:T(8,128)(2,1)} custom-call(bf16[1,384,2048]{2,1,0:T(8,128)(2,1)} %pool_hbm.1, s32[1,8,1,512]{3,2,1,0:T(1,128)} %index_hbm.1, bf16[1,2048,256]{2,1,0:T(8,128)(2,1)} %start_hbm.1, bf16[1,1,512,256]{3,2,1,0:T(8,128)(2,1)} %goal_hbm.1), custom_call_target="tpu_custom_call" | custom-call | tf_op jit(solution)/shard_map/pallas_call | solution.py:403
  62.4 2.3 %copy.6 = bf16[1,2048,256]{2,1,0:T(8,128)(2,1)} copy(bf16[1,2048,256]{2,1,0:T(8,128)(2,1)} %bitcast.1) | data formatting | bytes 2097152

commit v3 on v2

--- a/solution.py
+++ b/solution.py
@@ -19,7 +19,15 @@
 MESH = pl.DeviceIdType.MESH
 F32 = jnp.float32
 BF16 = jnp.bfloat16
-A_ROWS = 48
+PARTS = (48, 16)
+
+
+def hops(place):
+    i, j = place
+    return min(i, 4 - i) + min(j, RING - j)
+
+
+OTHERS = sorted(((i, j) for i in range(4) for j in range(RING) if i or j), key=hops, reverse=True)
 
 
 def dot(a, b):
@@ -104,12 +112,13 @@
     goal_ref,
     turned,
     delta,
-    recv,
+    recv_top,
+    recv_low,
     wide,
     operand,
     gram_pad,
-    gram_one,
-    gram_two,
+    gram_core,
+    gram_all,
     coefs,
     load_sem,
     a2a_send,
@@ -127,10 +136,11 @@
     yb_send,
     yb_recv,
 ):
-    halves, reps, half, cols = recv.shape
-    seg = halves * half
+    reps, _, cols = recv_top.shape
+    recv = (recv_top, recv_low)
+    starts = (0, PARTS[0])
+    seg = sum(PARTS)
     tall = reps // RING
-    pairs = tall * CUT
     me = lax.axis_index("rep")
     shard = lax.axis_index("shard")
     x = me // RING
@@ -153,26 +163,25 @@
 
     barrier = pltpu.get_barrier_semaphore()
 
-    def greet(k, carry):
+    def x_peer(i):
+        return lax.rem(x + i, tall)
+
+    def y_peer(j):
+        return lax.rem(y + j, RING)
+
+    def peer_at(place):
+        return x_peer(place[0]) * RING + y_peer(place[1])
+
+    for place in OTHERS:
         pl.semaphore_signal(
             barrier,
             inc=1,
-            device_id={"rep": lax.rem(me + k, reps), "shard": shard},
+            device_id={"rep": peer_at(place), "shard": shard},
             device_id_type=MESH,
         )
-        return carry
-
-    def greet_other(i, carry):
-        pl.semaphore_signal(
-            barrier,
-            inc=1,
-            device_id={"rep": lax.rem(x + i, tall) * RING + y, "shard": shard ^ 1},
-            device_id_type=MESH,
-        )
-        return carry
-
-    lax.fori_loop(1, reps, greet, 0)
-    lax.fori_loop(0, tall, greet_other, 0)
+    pl.semaphore_signal(
+        barrier, inc=1, device_id={"rep": me, "shard": shard ^ 1}, device_id_type=MESH
+    )
 
     def copy(src, dst, send_sem, recv_sem, rep, to_shard=None):
         return pltpu.make_async_remote_copy(
@@ -184,24 +193,18 @@
             device_id_type=MESH,
         )
 
-    def x_peer(i):
-        return lax.rem(x + i, tall)
-
-    def y_peer(j):
-        return lax.rem(y + j, RING)
-
     loads[0].wait()
     turned[...] = pool_ref[...].T
     for load in loads[1:]:
         load.wait()
     weights = local_steps(pool_ref[...], start_ref[...], index_ref[...], goal_ref[...])
 
-    pl.semaphore_wait(barrier, reps - 1 + tall)
+    pl.semaphore_wait(barrier, reps)
 
     def a2a(peer, h):
         return copy(
-            delta.at[pl.ds(pl.multiple_of(peer * seg + h * half, half), half), :],
-            recv.at[h, me],
+            delta.at[pl.ds(pl.multiple_of(peer * seg + starts[h], 16), PARTS[h]), :],
+            recv[h].at[me],
             a2a_send.at[0],
             a2a_recv.at[h],
             peer,
@@ -210,47 +213,42 @@
     def a2a_all(h):
         count = reps - 1
         return copy(
-            recv.at[h, pl.ds(0, count)],
-            recv.at[h, pl.ds(0, count)],
+            recv[h].at[pl.ds(0, count)],
+            recv[h].at[pl.ds(0, count)],
             a2a_send.at[0],
             a2a_recv.at[h],
             lax.rem(me + 1, reps),
         )
 
-    for i in range(tall):
-        to_x = x_peer(i)
-        block = pl.ds(pl.multiple_of(to_x * RING * seg, RING * seg), RING * seg)
-        delta[block, :] = dot(turned[block, :], weights).astype(BF16)
-
-        def send(j, carry, to_x=to_x):
-            a2a(to_x * RING + y_peer(j), 0).start()
-            return carry
-
-        lax.fori_loop(1 if i == 0 else 0, RING, send, 0)
-
-    def send_rest(k, carry):
-        a2a(lax.rem(me + k, reps), 1).start()
-        return carry
-
-    lax.fori_loop(1, reps, send_rest, 0)
-    for h in range(halves):
-        own = pl.ds(pl.multiple_of(me * seg + h * half, half), half)
-        recv[h, me] = delta[own, :]
+    order = (4, 1, 7, 3, 5, 2, 6, 0)
+    for h in range(len(PARTS)):
+        for i in (2, 1, 3, 0):
+            if h == 0:
+                block = pl.ds(pl.multiple_of(x_peer(i) * RING * seg, RING * seg), RING * seg)
+                delta[block, :] = dot(turned[block, :], weights).astype(BF16)
+            for j in order:
+                if i or j:
+                    a2a(peer_at((i, j)), h).start()
+
+    def own(h):
+        return pl.ds(pl.multiple_of(me * seg + starts[h], 16), PARTS[h])
 
     gram = None
-    for h in range(halves):
+    for h, rows in enumerate(PARTS):
+        recv[h][me] = delta[own(h), :]
         a2a_all(h).wait_recv()
         for q in range(reps):
             for c in range(cols // 128):
-                wide[c, half * q : half * q + half, :] = recv[
-                    h, q, :, 128 * c : 128 * c + 128
+                wide[c, rows * q : rows * q + rows, :] = recv[h][
+                    q, :, 128 * c : 128 * c + 128
                 ].astype(F32)
-        for r in range(half):
+        for r in range(rows):
             for c in range(cols // 128):
-                part = wide[c, pl.ds(r, reps, stride=half), :]
+                part = wide[c, pl.ds(r, reps, stride=rows), :]
                 place = r * cols + 128 * c
                 operand[:, place : place + 128] = part.astype(BF16)
-        term = dot_last(operand[...], operand[...])
+        sides = operand[:, 0 : rows * cols]
+        term = dot_last(sides, sides)
         gram = term if gram is None else gram + term
 
     gram_pad[...] = jnp.zeros_like(gram_pad)
@@ -259,39 +257,34 @@
     for k in range(1, reps // 8):
         packed = packed + pltpu.roll(gram_pad[8 * k : 8 * k + 8, :], reps * k, 1)
 
-    mine = x * CUT + core
-    gram_one[mine] = packed
-
-    def one(k, arriving):
-        peer = lax.rem(mine + k, pairs)
-        place = peer if arriving else mine
-        return copy(
-            gram_one.at[mine],
-            gram_one.at[place],
-            one_send.at[peer],
-            one_recv.at[place],
-            (peer // CUT) * RING + y,
-            (shard // CUT) * CUT + peer % CUT,
-        )
-
-    def two(j, arriving):
-        p = y_peer(j)
-        place = p if arriving else y
-        return copy(
-            gram_two.at[y], gram_two.at[place], two_send.at[p], two_recv.at[place], x * RING + p
-        )
-
-    far_first = (4, 3, 5, 2, 6, 1, 7)
-    for k in range(1, pairs):
-        one(k, False).start()
-    for k in range(1, pairs):
-        one(k, True).wait_recv()
-    gram_two[y] = jnp.sum(gram_one[...], axis=0)
-    for j in far_first:
-        two(j, False).start()
-    for j in range(1, RING):
-        two(j, True).wait_recv()
-    packed = jnp.sum(gram_two[...], axis=0)
+    gram_core[core] = packed
+
+    def one(place):
+        return copy(
+            gram_core.at[core],
+            gram_core.at[place],
+            one_send.at[0],
+            one_recv.at[0],
+            me,
+            shard ^ 1,
+        )
+
+    def two(place):
+        return copy(
+            gram_all.at[me], gram_all.at[me], two_send.at[0], two_recv.at[0], peer_at(place)
+        )
+
+    def two_all():
+        every = gram_all.at[pl.ds(0, reps - 1)]
+        return copy(every, every, two_send.at[0], two_recv.at[0], peer_at(OTHERS[0]))
+
+    one(core).start()
+    one(1 - core).wait_recv()
+    gram_all[me] = gram_core[0] + gram_core[1]
+    for place in OTHERS:
+        two(place).start()
+    two_all().wait_recv()
+    packed = jnp.sum(gram_all[...], axis=0)
     lane = lax.broadcasted_iota(jnp.int32, packed.shape, 1)
     pieces = [
         jnp.where(lane < reps, packed if k == 0 else pltpu.roll(packed, 128 - reps * k, 1), 0.0)
@@ -300,18 +293,17 @@
     coef = tree_coefs(jnp.concatenate(pieces, axis=0))
     coefs[...] = jnp.broadcast_to(coef, coefs.shape)
 
-    for h in range(halves):
-        total = jnp.zeros((half, cols), F32)
+    def finish(h):
+        total = jnp.zeros((PARTS[h], cols), F32)
         for q in range(reps):
-            total = total + coefs[q : q + 1, :] * recv[h, q].astype(F32)
-        rows = pl.ds(pl.multiple_of(me * seg + h * half, half), half)
+            total = total + coefs[q : q + 1, :] * recv[h][q].astype(F32)
         combined = total.astype(BF16).astype(F32)
-        out_ref[x, y, half * h : half * h + half] = (
-            start_ref[rows, :].astype(F32) + combined
+        out_ref[x, y, starts[h] : starts[h] + PARTS[h]] = (
+            start_ref[own(h), :].astype(F32) + combined
         ).astype(BF16)
 
-    top = pl.ds(0, A_ROWS)
-    low = pl.ds(A_ROWS, seg - A_ROWS)
+    top = pl.ds(0, PARTS[0])
+    low = pl.ds(PARTS[0], PARTS[1])
 
     def ya(j, arriving):
         p = y_peer(j)
@@ -358,9 +350,12 @@
         )
 
     near_first = (1, 7, 2, 6, 3, 5, 4)
+    far_first = (4, 3, 5, 2, 6, 1, 7)
     across = (2, 1, 3)
+    finish(1)
     for i in across:
         xb(i, False).start()
+    finish(0)
     for j in near_first:
         ya(j, False).start()
     for i in across:
@@ -378,12 +373,11 @@
     for i in range(1, tall):
         xa_all(i).wait_recv()
 
-    for h in range(halves):
+    for h in range(len(PARTS)):
         a2a_all(h).wait_send()
-    for k in range(1, pairs):
-        one(k, False).wait_send()
+    one(core).wait_send()
+    two_all().wait_send()
     for j in range(1, RING):
-        two(j, False).wait_send()
         ya(j, False).wait_send()
         yb(j, False).wait_send()
     for i in range(1, tall):
@@ -398,7 +392,6 @@
     total = row_index.shape[3]
     cols = weights.shape[2]
     seg = width // reps
-    half = seg // 2
     dma = pltpu.SemaphoreType.DMA
     out = pl.pallas_call(
         kernel,
@@ -412,20 +405,21 @@
             pltpu.VMEM((total, cols), BF16),
             pltpu.VMEM((width, pool_count), BF16),
             pltpu.VMEM((width, cols), BF16),
-            pltpu.VMEM((2, reps, half, cols), BF16),
-            pltpu.VMEM((cols // 128, reps * half, 128), F32),
-            pltpu.VMEM((reps, half * cols), BF16),
+            pltpu.VMEM((reps, PARTS[0], cols), BF16),
+            pltpu.VMEM((reps, PARTS[1], cols), BF16),
+            pltpu.VMEM((cols // 128, reps * PARTS[0], 128), F32),
+            pltpu.VMEM((reps, PARTS[0] * cols), BF16),
             pltpu.VMEM((reps, 128), F32),
-            pltpu.VMEM((tall * CUT, 8, 128), F32),
-            pltpu.VMEM((RING, 8, 128), F32),
+            pltpu.VMEM((CUT, 8, 128), F32),
+            pltpu.VMEM((reps, 8, 128), F32),
             pltpu.VMEM((reps, cols), F32),
             dma((4,)),
             dma((1,)),
             dma((2,)),
-            dma((tall * CUT,)),
-            dma((tall * CUT,)),
-            dma((RING,)),
-            dma((RING,)),
+            dma((1,)),
+            dma((1,)),
+            dma((1,)),
+            dma((1,)),
             dma((RING,)),
             dma((RING,)),
             dma((tall,)),
@@ -436,9 +430,14 @@
             dma((RING,)),
         ],
         compiler_params=pltpu.CompilerParams(
-            collective_id=0, has_side_effects=True, vmem_limit_bytes=60 * 1024 * 1024
+            collective_id=0, has_side_effects=True, vmem_limit_bytes=40 * 1024 * 1024
         ),
-    )(token_pool, row_index, weights, targets)
+    )(
+        *(
+            pltpu.with_memory_space_constraint(array, pltpu.HBM)
+            for array in (token_pool, row_index, weights, targets)
+        )
+    )
     return out.reshape(weights.shape)
 
 

time: 64.8 us -> 59.8 us (0.923)
  the two profiles are of different devices: /device:TPU:394 before, /device:TPU:448 now
where the time goes in v3:
time: 59.8 us; the launch traced here: 58.7 us
  Pallas kernels  57.7 us (96%)
  local copies, waits for them, and re-layouts  0.97 us (2%)
    pallas_call x1, Pallas kernels, body(): pl.pallas_call(kernel, out_shape=jax.ShapeDtypeStruct((tall, RING, seg, c...  57.7 us

profile of v3, /device:TPU:448, one launch (start us, length us, event | category | flops | bytes accessed | tf_op | source)
XLA Modules:
  0.0 58.7 jit_solution(9649801394853871662)
XLA Ops:
  0.0 57.7 %shard_map.46 = bf16[4,8,64,256]{3,2,1,0:T(8,128)(2,1)S(1)} custom-call(bf16[1,384,2048]{2,1,0:T(8,128)(2,1)} %pool_hbm.1, s32[1,8,1,512]{3,2,1,0:T(1,128)} %index_hbm.1, bf16[1,2048,256]{2,1,0:T(8,128)(2,1)} %start_hbm.1, bf16[1,1,512,256]{3,2,1,0:T(8,128)(2,1)} %goal_hbm.1), custom_call_target="tpu_custom_call" | custom-call | tf_op jit(solution)/shard_map/pallas_call | solution.py:396
  57.7 1.0 %copy.6 = bf16[1,2048,256]{2,1,0:T(8,128)(2,1)} copy(bf16[1,2048,256]{2,1,0:T(8,128)(2,1)S(1)} %bitcast.1) | data formatting | bytes 2097152

commit v4 on v3

--- a/solution.py
+++ b/solution.py
@@ -20,6 +20,7 @@
 F32 = jnp.float32
 BF16 = jnp.bfloat16
 PARTS = (48, 16)
+LOADS = 4
 
 
 def hops(place):
@@ -42,34 +43,41 @@
     return lax.dot_general(a, b, (((0,), (0,)), ((), ())), preferred_element_type=F32)
 
 
-def local_steps(pool, start, picked, goals):
-    pool_count, width = pool.shape
-    total = picked.shape[1]
-    rows = total // STEPS
+def routing(picked, pool_count):
+    slots = lax.broadcasted_iota(jnp.int32, (pool_count, picked.shape[1]), 0)
+    marks = jnp.where(slots == picked, 1.0, 0.0)
+    return marks.astype(BF16), marks.T.astype(BF16)
+
+
+def local_steps(first, products, marks, picks, goals, width, gates):
+    rows = marks.shape[1] // STEPS
     inv_width = 1.0 / math.sqrt(width)
     scale = LEARN_RATE / math.sqrt(rows)
-    first = dot(pool, start)
-    kernel_matrix = dot_last(pool, pool).astype(BF16)
-    slots = lax.broadcasted_iota(jnp.int32, (pool_count, total), 0)
-    marks = (slots == picked).astype(BF16)
-    z = first
-    velocity = None
+    reach = [sum(MOMENTUM**k for k in range(n)) for n in range(STEPS + 1)]
+    high = first.astype(BF16)
+    low = (first - high.astype(F32)).astype(BF16)
+    base = (dot(picks, high) + dot(picks, low)) * inv_width
+    routed = dot(picks[rows:], products.astype(BF16)).astype(BF16)
     moved = None
     for step in range(STEPS):
-        mark = marks[:, step * rows : (step + 1) * rows]
-        high = z.astype(BF16)
-        low = (z - high.astype(F32)).astype(BF16)
-        hidden = (dot_first(mark, high) + dot_first(mark, low)) * inv_width
+        block = slice(step * rows, (step + 1) * rows)
+        hidden = base[block]
+        if step:
+            met = dot(routed[(step - 1) * rows : step * rows], marks[:, 0 : step * rows])
+            parts = [
+                met[:, s * rows : (s + 1) * rows] * (-scale * inv_width * reach[step - s])
+                for s in range(step)
+            ]
+            met = jnp.concatenate(parts, axis=1).astype(BF16)
+            hidden = hidden + dot(met, gates[0 : step * rows, :])
         sigma = jax.nn.sigmoid(hidden)
         slope = sigma * (1.0 + hidden * (1.0 - sigma))
-        wanted = goals[step * rows : (step + 1) * rows].astype(F32)
+        wanted = goals[block].astype(F32)
         grad_hidden = ((hidden * sigma - wanted) * slope).astype(BF16)
-        spread = dot(mark, grad_hidden)
-        velocity = spread if velocity is None else MOMENTUM * velocity + spread
-        moved = velocity if moved is None else moved + velocity
-        if step < STEPS - 1:
-            z = first - scale * dot(kernel_matrix, moved.astype(BF16))
-    return (-scale * moved).astype(BF16)
+        gates[block, :] = grad_hidden
+        term = dot(marks[:, block], grad_hidden) * (-scale * reach[STEPS - step])
+        moved = term if moved is None else moved + term
+    return moved.astype(BF16)
 
 
 def tree_coefs(gram):
@@ -110,6 +118,7 @@
     index_ref,
     start_ref,
     goal_ref,
+    gates,
     turned,
     delta,
     recv_top,
@@ -147,19 +156,25 @@
     y = me % RING
     core = shard % CUT
 
-    loads = [
-        pltpu.make_async_copy(src, dst, load_sem.at[k])
-        for k, (src, dst) in enumerate(
+    pool_count, width = pool_ref.shape
+    span = width // LOADS
+
+    def load(src, dst, k):
+        started = pltpu.make_async_copy(src, dst, load_sem.at[k])
+        started.start()
+        return started
+
+    index_load = load(index_hbm.at[0, pl.ds(shard // CUT, 1), 0], index_ref, 0)
+    loads = []
+    for k in range(LOADS):
+        part = pl.ds(k * span, span)
+        loads.append(
             (
-                (pool_hbm.at[0], pool_ref),
-                (start_hbm.at[0], start_ref),
-                (index_hbm.at[0, pl.ds(shard // CUT, 1), 0], index_ref),
-                (goal_hbm.at[0, 0], goal_ref),
+                load(pool_hbm.at[0, :, part], pool_ref.at[:, part], 2 + 2 * k),
+                load(start_hbm.at[0, part], start_ref.at[part], 3 + 2 * k),
             )
         )
-    ]
-    for load in loads:
-        load.start()
+    goal_load = load(goal_hbm.at[0, 0], goal_ref, 1)
 
     barrier = pltpu.get_barrier_semaphore()
 
@@ -193,11 +208,20 @@
             device_id_type=MESH,
         )
 
-    loads[0].wait()
-    turned[...] = pool_ref[...].T
-    for load in loads[1:]:
-        load.wait()
-    weights = local_steps(pool_ref[...], start_ref[...], index_ref[...], goal_ref[...])
+    index_load.wait()
+    marks, picks = routing(index_ref[...], pool_count)
+    first = products = None
+    for k in range(LOADS):
+        for part in loads[k]:
+            part.wait()
+        tokens = pool_ref[:, k * span : (k + 1) * span]
+        turned[k * span : (k + 1) * span, :] = tokens.T
+        one_first = dot(tokens, start_ref[k * span : (k + 1) * span, :])
+        one_products = dot_last(tokens, tokens)
+        first = one_first if first is None else first + one_first
+        products = one_products if products is None else products + one_products
+    goal_load.wait()
+    weights = local_steps(first, products, marks, picks, goal_ref, width, gates)
 
     pl.semaphore_wait(barrier, reps)
 
@@ -403,6 +427,7 @@
             pltpu.VMEM((1, total), jnp.int32),
             pltpu.VMEM((width, cols), BF16),
             pltpu.VMEM((total, cols), BF16),
+            pltpu.VMEM((total, cols), BF16),
             pltpu.VMEM((width, pool_count), BF16),
             pltpu.VMEM((width, cols), BF16),
             pltpu.VMEM((reps, PARTS[0], cols), BF16),
@@ -413,7 +438,7 @@
             pltpu.VMEM((CUT, 8, 128), F32),
             pltpu.VMEM((reps, 8, 128), F32),
             pltpu.VMEM((reps, cols), F32),
-            dma((4,)),
+            dma((2 + 2 * LOADS,)),
             dma((1,)),
             dma((2,)),
             dma((1,)),

time: 59.8 us -> 59.2 us (0.990)
  no operation moved by 1% of the time
where the time goes in v4:
time: 59.2 us; the launch traced here: 58.3 us
  Pallas kernels  57.3 us (97%)
  local copies, waits for them, and re-layouts  0.97 us (2%)
    pallas_call x1, Pallas kernels, body(): pl.pallas_call(kernel, out_shape=jax.ShapeDtypeStruct((tall, RING, seg, c...  57.3 us

profile of v4, /device:TPU:448, one launch (start us, length us, event | category | flops | bytes accessed | tf_op | source)
XLA Modules:
  0.0 58.3 jit_solution(2883443043024322905)
XLA Ops:
  0.0 57.3 %shard_map.46 = bf16[4,8,64,256]{3,2,1,0:T(8,128)(2,1)S(1)} custom-call(bf16[1,384,2048]{2,1,0:T(8,128)(2,1)} %pool_hbm.1, s32[1,8,1,512]{3,2,1,0:T(1,128)} %index_hbm.1, bf16[1,2048,256]{2,1,0:T(8,128)(2,1)} %start_hbm.1, bf16[1,1,512,256]{3,2,1,0:T(8,128)(2,1)} %goal_hbm.1), custom_call_target="tpu_custom_call" | custom-call | tf_op jit(solution)/shard_map/pallas_call | solution.py:420
  57.3 1.0 %copy.6 = bf16[1,2048,256]{2,1,0:T(8,128)(2,1)} copy(bf16[1,2048,256]{2,1,0:T(8,128)(2,1)S(1)} %bitcast.1) | data formatting | bytes 2097152

commit v5 on v4

--- a/solution.py
+++ b/solution.py
@@ -20,6 +20,7 @@
 F32 = jnp.float32
 BF16 = jnp.bfloat16
 PARTS = (48, 16)
+FORWARD = 6
 LOADS = 4
 
 
@@ -362,48 +363,63 @@
             p * RING + y,
         )
 
-    def yb(j, arriving):
-        p = y_peer(j)
-        place = p if arriving else y
-        return copy(
-            out_ref.at[:, y, low],
-            out_ref.at[:, place, low],
-            yb_send.at[p],
-            yb_recv.at[place],
-            x * RING + p,
-        )
+    def yb(k, to_j, from_j, some=slice(None)):
+        chunk = out_ref.at[some, y_peer(from_j), low]
+        place = y_peer(from_j)
+        return copy(chunk, chunk, yb_send.at[k], yb_recv.at[place], x * RING + y_peer(to_j))
+
+    def yb_hops():
+        first = [yb(k, j, 0) for k, j in enumerate((2, 6, 1, 7))]
+        side = tall // 2
+        second = [
+            yb(4, 1, 6),
+            yb(5, 7, 2),
+            yb(6, 2, 6, pl.ds(0, side)),
+            yb(7, 6, 2, pl.ds(side, tall - side)),
+        ]
+        return first, second
+
+    def yb_arrive(j):
+        yb(0, j, j).wait_recv()
 
     near_first = (1, 7, 2, 6, 3, 5, 4)
-    far_first = (4, 3, 5, 2, 6, 1, 7)
     across = (2, 1, 3)
-    finish(1)
-    for i in across:
-        xb(i, False).start()
     finish(0)
     for j in near_first:
         ya(j, False).start()
     for i in across:
         xa(i, 0).start()
-    for i in range(1, tall):
-        xb(i, True).wait_recv()
-    for j in far_first:
-        yb(j, False).start()
-    for j in near_first:
+    finish(1)
+    for i in across:
+        xb(i, False).start()
+    for n, j in enumerate(near_first):
         ya(j, True).wait_recv()
         for i in across:
             xa(i, j).start()
-    for j in range(1, RING):
-        yb(j, True).wait_recv()
+        if n == 1:
+            for i in range(1, tall):
+                xb(i, True).wait_recv()
+            for hop in yb_hops()[0]:
+                hop.start()
+        if n == FORWARD:
+            yb_arrive(6)
+            yb_arrive(2)
+            for hop in yb_hops()[1]:
+                hop.start()
+    for j in (1, 7, 3, 5, 4):
+        yb_arrive(j)
     for i in range(1, tall):
         xa_all(i).wait_recv()
 
     for h in range(len(PARTS)):
         a2a_all(h).wait_send()
+    for hops_made in yb_hops():
+        for hop in hops_made:
+            hop.wait_send()
     one(core).wait_send()
     two_all().wait_send()
     for j in range(1, RING):
         ya(j, False).wait_send()
-        yb(j, False).wait_send()
     for i in range(1, tall):
         xa_all(i).wait_send()
         xb(i, False).wait_send()
@@ -432,7 +448,7 @@
             pltpu.VMEM((width, cols), BF16),
             pltpu.VMEM((reps, PARTS[0], cols), BF16),
             pltpu.VMEM((reps, PARTS[1], cols), BF16),
-            pltpu.VMEM((cols // 128, reps * PARTS[0], 128), F32),
+            pltpu.VMEM((cols // 128, (reps + 1) * PARTS[0], 128), F32),
             pltpu.VMEM((reps, PARTS[0] * cols), BF16),
             pltpu.VMEM((reps, 128), F32),
             pltpu.VMEM((CUT, 8, 128), F32),

time: 59.2 us -> 59.2 us (level)
  no operation moved by 1% of the time
where the time goes in v5:
time: 59.2 us; the launch traced here: 58.7 us
  Pallas kernels  57.7 us (97%)
  local copies, waits for them, and re-layouts  0.97 us (2%)
    pallas_call x1, Pallas kernels, body(): pl.pallas_call(kernel, out_shape=jax.ShapeDtypeStruct((tall, RING, seg, c...  57.7 us

profile of v5, /device:TPU:448, one launch (start us, length us, event | category | flops | bytes accessed | tf_op | source)
XLA Modules:
  0.0 58.7 jit_solution(18067505766929250106)
XLA Ops:
  0.0 57.7 %shard_map.46 = bf16[4,8,64,256]{3,2,1,0:T(8,128)(2,1)S(1)} custom-call(bf16[1,384,2048]{2,1,0:T(8,128)(2,1)} %pool_hbm.1, s32[1,8,1,512]{3,2,1,0:T(1,128)} %index_hbm.1, bf16[1,2048,256]{2,1,0:T(8,128)(2,1)} %start_hbm.1, bf16[1,1,512,256]{3,2,1,0:T(8,128)(2,1)} %goal_hbm.1), custom_call_target="tpu_custom_call" | custom-call | tf_op jit(solution)/shard_map/pallas_call | solution.py:436
  57.8 1.0 %copy.6 = bf16[1,2048,256]{2,1,0:T(8,128)(2,1)} copy(bf16[1,2048,256]{2,1,0:T(8,128)(2,1)S(1)} %bitcast.1) | data formatting | bytes 2097152

commit v6 on v4

--- a/solution.py
+++ b/solution.py
@@ -432,7 +432,7 @@
             pltpu.VMEM((width, cols), BF16),
             pltpu.VMEM((reps, PARTS[0], cols), BF16),
             pltpu.VMEM((reps, PARTS[1], cols), BF16),
-            pltpu.VMEM((cols // 128, reps * PARTS[0], 128), F32),
+            pltpu.VMEM((cols // 128, (reps + 1) * PARTS[0], 128), F32),
             pltpu.VMEM((reps, PARTS[0] * cols), BF16),
             pltpu.VMEM((reps, 128), F32),
             pltpu.VMEM((CUT, 8, 128), F32),

time: 59.2 us -> 59.2 us (level)
  no operation moved by 1% of the time
where the time goes in v6:
time: 59.2 us; the launch traced here: 58.3 us
  Pallas kernels  57.3 us (97%)
  local copies, waits for them, and re-layouts  0.97 us (2%)
    pallas_call x1, Pallas kernels, body(): pl.pallas_call(kernel, out_shape=jax.ShapeDtypeStruct((tall, RING, seg, c...  57.3 us

profile of v6, /device:TPU:448, one launch (start us, length us, event | category | flops | bytes accessed | tf_op | source)
XLA Modules:
  0.0 58.3 jit_solution(17605151439529163661)
XLA Ops:
  0.0 57.3 %shard_map.46 = bf16[4,8,64,256]{3,2,1,0:T(8,128)(2,1)S(1)} custom-call(bf16[1,384,2048]{2,1,0:T(8,128)(2,1)} %pool_hbm.1, s32[1,8,1,512]{3,2,1,0:T(1,128)} %index_hbm.1, bf16[1,2048,256]{2,1,0:T(8,128)(2,1)} %start_hbm.1, bf16[1,1,512,256]{3,2,1,0:T(8,128)(2,1)} %goal_hbm.1), custom_call_target="tpu_custom_call" | custom-call | tf_op jit(solution)/shard_map/pallas_call | solution.py:420
  57.3 1.0 %copy.6 = bf16[1,2048,256]{2,1,0:T(8,128)(2,1)} copy(bf16[1,2048,256]{2,1,0:T(8,128)(2,1)S(1)} %bitcast.1) | data formatting | bytes 2097152

commit v7 on v6

--- a/solution.py
+++ b/solution.py
@@ -210,16 +210,21 @@
 
     index_load.wait()
     marks, picks = routing(index_ref[...], pool_count)
-    first = products = None
+    first = square = border = None
+    cut = 2 * pool_count // 3
     for k in range(LOADS):
         for part in loads[k]:
             part.wait()
         tokens = pool_ref[:, k * span : (k + 1) * span]
         turned[k * span : (k + 1) * span, :] = tokens.T
         one_first = dot(tokens, start_ref[k * span : (k + 1) * span, :])
-        one_products = dot_last(tokens, tokens)
+        one_square = dot_last(tokens[:cut], tokens[:cut])
+        one_border = dot_last(tokens[cut:], tokens)
         first = one_first if first is None else first + one_first
-        products = one_products if products is None else products + one_products
+        square = one_square if square is None else square + one_square
+        border = one_border if border is None else border + one_border
+    upper = jnp.concatenate([square, border[:, :cut].T], axis=1)
+    products = jnp.concatenate([upper, border], axis=0)
     goal_load.wait()
     weights = local_steps(first, products, marks, picks, goal_ref, width, gates)
 

time: 59.2 us -> 58.9 us (level)
  no operation moved by 1% of the time
where the time goes in v7:
time: 58.9 us; the launch traced here: 58.3 us
  Pallas kernels  57.3 us (97%)
  local copies, waits for them, and re-layouts  0.97 us (2%)
    pallas_call x1, Pallas kernels, body(): pl.pallas_call(kernel, out_shape=jax.ShapeDtypeStruct((tall, RING, seg, c...  57.3 us

profile of v7, /device:TPU:448, one launch (start us, length us, event | category | flops | bytes accessed | tf_op | source)
XLA Modules:
  0.0 58.3 jit_solution(9877112832633406118)
XLA Ops:
  0.0 57.3 %shard_map.46 = bf16[4,8,64,256]{3,2,1,0:T(8,128)(2,1)S(1)} custom-call(bf16[1,384,2048]{2,1,0:T(8,128)(2,1)} %pool_hbm.1, s32[1,8,1,512]{3,2,1,0:T(1,128)} %index_hbm.1, bf16[1,2048,256]{2,1,0:T(8,128)(2,1)} %start_hbm.1, bf16[1,1,512,256]{3,2,1,0:T(8,128)(2,1)} %goal_hbm.1), custom_call_target="tpu_custom_call" | custom-call | tf_op jit(solution)/shard_map/pallas_call | solution.py:425
  57.3 1.0 %copy.6 = bf16[1,2048,256]{2,1,0:T(8,128)(2,1)} copy(bf16[1,2048,256]{2,1,0:T(8,128)(2,1)S(1)} %bitcast.1) | data formatting | bytes 2097152
